TPU v7x, 256 devices: a whole 4x4x8 slice. The times are simulated.
256 devices in a mesh: pipe: 4 (over y), dp: 32 (over z, x), tensor: 2 (over core).
Axes of the slice: x: 4, y: 4, z: 8, core: 2. Of those that a mesh axis runs over, the one named last changes fastest.
Arguments:
- llm_grad: bfloat16 [4, 1024, 1664], P(None, 'dp'), may hold values from -6 to 6
- slot_row: int32 [4, 32, 32], P(None, 'dp'), may hold values from 0 to 31, each once within a row
- counts: int32 [32, 4], P('dp'), may hold values from 8 to 32, as said below
- saved_in: bfloat16 [4, 4, 1024, 1664], P('pipe', None, 'dp'), may hold values from -6 to 6
- saved_pre: bfloat16 [4, 4, 1024, 6400], P('pipe', None, 'dp', 'tensor'), may hold values from -6 to 6
- weights: bfloat16 [4, 1664, 6400], P('pipe', 'dp', 'tensor'), may hold values from -0.15625 to 0.15625
- channel_scale: float32 [4, 1664], P('pipe'), may hold values from 0.25 to 2
Outputs:
- weight_grad: bfloat16 [4, 1664, 6400], P('pipe', 'dp', 'tensor')
- section_grad: bfloat16 [4, 4, 1024, 1664], P('pipe', None, 'dp')
Inputs may be any that keep to these rules, and one draw needn't show every extreme that they name: For each micro-batch and rank, slot_row lists every row of the rank once. `counts`: both ends of the range occur in every draw.
All inputs are finite; a program needn't handle non-finite values.
Results may differ from a plain program's by a relative error of at most 0.023.
Values may be sent and summed in bfloat16 or wider, within the bound.
A program may use at most 128 MiB of HBM per device.

v0:
```python
import jax
import jax.numpy as jnp
from jax import lax
from jax.sharding import PartitionSpec as P

norm_eps = 1e-06
root_half = 0.7071067811865476
inv_root_two_pi = 0.3989422804014327


def shortened(value):

    def short(part):
        return part.astype(jnp.bfloat16) if part.dtype == jnp.float32 else part

    return jax.tree.map(short, value)


def shifted(block, axis, distance):
    devices = range(lax.axis_size(axis))
    route = [(i - distance, i) for i in devices if i - distance in devices]
    return lax.ppermute(block, axis, route)


def gelu_parts(pre_act):
    normal_cdf = 0.5 * (1.0 + jax.scipy.special.erf(pre_act * root_half))
    density = jnp.exp(-0.5 * pre_act * pre_act) * inv_root_two_pi
    return (pre_act * normal_cdf, normal_cdf + pre_act * density)


def local_top(llm_grad, slot_row, counts):
    row_count = llm_grad.shape[1]
    slot_ids = jnp.arange(row_count, dtype=jnp.int32)
    kept_mask = slot_ids[None, :] < counts[:, None]
    source = jnp.where(kept_mask[..., None], llm_grad, jnp.zeros_like(llm_grad))
    onehot = (slot_row[:, :, None] == slot_ids[None, None, :]).astype(jnp.bfloat16)
    placed = jnp.einsum("mjr,mjd->mrd", onehot, source, preferred_element_type=jnp.float32)
    return placed.astype(jnp.bfloat16)


def norm_back(incoming, dnorm, unit_rows, inv_std, channel_gain):
    scaled_back = dnorm * channel_gain
    back = inv_std * (
        scaled_back
        - jnp.mean(scaled_back, axis=-1, keepdims=True)
        - unit_rows * jnp.mean(scaled_back * unit_rows, axis=-1, keepdims=True)
    )
    return (incoming.astype(jnp.float32) + back).astype(jnp.bfloat16)


def add_term(grad_total, left_side, right_side):
    return grad_total + lax.dot_general(
        left_side, right_side, (((0,), (0,)), ((), ())), preferred_element_type=jnp.float32
    )


def keep_total(grad_total, left_side, right_side):
    return grad_total


def body(llm_grad, slot_row, counts, saved_in, saved_pre, weights, channel_scale):
    sections = lax.axis_size("pipe")
    section_index = lax.axis_index("pipe")
    micro_count = llm_grad.shape[0]
    row_count = llm_grad.shape[1]
    model_width = llm_grad.shape[2]
    hidden = saved_pre.shape[3]
    is_up = section_index % 2 == 0
    is_top = section_index == sections - 1
    full_weight = lax.all_gather(weights[0], "dp", axis=0, tiled=True)
    channel_gain = channel_scale[0]
    top_grad = local_top(llm_grad, slot_row[:, 0], counts[0])
    zero_wide = jnp.zeros((row_count, model_width), jnp.float32)
    zero_narrow = jnp.zeros((row_count, model_width), jnp.bfloat16)
    zero_hidden = jnp.zeros((row_count, hidden), jnp.bfloat16)

    def spare_work(incoming, hidden_in, inputs, pre_act):
        return (zero_wide, zero_hidden, zero_narrow, zero_hidden)

    def down_work(incoming, hidden_in, inputs, pre_act):
        scaled = (incoming.astype(jnp.float32) * channel_gain).astype(jnp.bfloat16)
        hidden_grad = jnp.dot(scaled, full_weight, preferred_element_type=jnp.float32).astype(
            jnp.bfloat16
        )
        activated = gelu_parts(pre_act.astype(jnp.float32))[0].astype(jnp.bfloat16)
        return (zero_wide, hidden_grad, scaled, activated)

    def up_work(incoming, hidden_in, inputs, pre_act):
        act_grad = (
            hidden_in.astype(jnp.float32) * gelu_parts(pre_act.astype(jnp.float32))[1]
        ).astype(jnp.bfloat16)
        values = inputs.astype(jnp.float32)
        center = values - jnp.mean(values, axis=-1, keepdims=True)
        inv_std = lax.rsqrt(jnp.mean(center * center, axis=-1, keepdims=True) + norm_eps)
        normed = (center * inv_std * channel_gain).astype(jnp.bfloat16)
        partial_value = lax.dot_general(
            act_grad, full_weight, (((1,), (1,)), ((), ())), preferred_element_type=jnp.float32
        )
        return (partial_value, zero_hidden, normed, act_grad)

    def advance(loop_state, tick_index):
        grad_store, out_buffer, recv_hidden, recv_res = loop_state
        micro_index = tick_index - (sections - 1 - section_index)
        is_valid = (micro_index >= 0) & (micro_index < micro_count)
        micro_safe = jnp.clip(micro_index, 0, micro_count - 1)
        incoming = jnp.where(is_top, top_grad[micro_safe], recv_res)
        inputs = saved_in[0, micro_safe]
        pre_act = saved_pre[0, micro_safe]
        branch = jnp.where(is_valid, jnp.where(is_up, 2, 1), 0).astype(jnp.int32)
        partial_value, hidden_out, left_side, right_side = lax.switch(
            branch, [spare_work, down_work, up_work], incoming, recv_hidden, inputs, pre_act
        )
        values = inputs.astype(jnp.float32)
        center = values - jnp.mean(values, axis=-1, keepdims=True)
        inv_std = lax.rsqrt(jnp.mean(center * center, axis=-1, keepdims=True) + norm_eps)
        unit_rows = center * inv_std
        summed = jax.tree.map(
            lambda part: part.astype(jnp.float32), lax.psum(shortened(partial_value), "tensor")
        )
        back_out = norm_back(incoming, summed, unit_rows, inv_std, channel_gain)
        outgoing = jnp.where(is_up, back_out, incoming)
        write_at = jnp.where(is_valid, micro_safe, micro_count)
        out_buffer = lax.dynamic_update_index_in_dim(out_buffer, outgoing, write_at, 0)
        grad_store = lax.cond(is_valid, add_term, keep_total, grad_store, left_side, right_side)
        recv_hidden, recv_res = (
            shifted(shortened(hidden_out), "pipe", -1).astype(hidden_out.dtype),
            shifted(outgoing, "pipe", -1),
        )
        return ((grad_store, out_buffer, recv_hidden, recv_res), None)

    grad_store = jnp.zeros((model_width, hidden), jnp.float32)
    out_buffer = jnp.zeros((micro_count + 1, row_count, model_width), jnp.bfloat16)
    tick_count = micro_count + sections - 1
    loop_state = (grad_store, out_buffer, zero_hidden, zero_narrow)
    loop_state, unused = lax.scan(advance, loop_state, jnp.arange(tick_count, dtype=jnp.int32))
    grad_store, out_buffer, recv_hidden, recv_res = loop_state
    weight_out = lax.psum_scatter(
        grad_store.astype(jnp.bfloat16), "dp", scatter_dimension=0, tiled=True
    )
    return (weight_out[None], out_buffer[:micro_count][None])


def solution(mesh):
    in_specs = (
        P(None, "dp", None),
        P(None, "dp", None),
        P("dp", None),
        P("pipe", None, "dp", None),
        P("pipe", None, "dp", "tensor"),
        P("pipe", "dp", "tensor"),
        P("pipe", None),
    )
    out_specs = (P("pipe", "dp", "tensor"), P("pipe", None, "dp", None))
    return jax.shard_map(body, mesh=mesh, in_specs=in_specs, out_specs=out_specs, check_vma=False)
```

profile of v0, /device:TPU:160, one launch (start us, length us, event | category | flops | bytes accessed | tf_op | source)
XLA Modules:
  0.0 917.6 jit_solution(5709121995667591268)
XLA Ops:
  7.2 2.4 copy.10
  10.3 1.4 convolution_convert_fusion.1
  11.7 160.9 %all-gather.3.cloned.1.call-done = bf16[1,1664,3200]{2,0,1:T(2,128)(2,1)} async-done(((bf16[1,52,3200]{2,0,1:T(2,128)(2,1)}), bf16[1,1664,3200]{2,0,1:T(2,128)(2,1)}) %all-gather.3.cloned.1.call-update) | async-done | bytes 10649616 | tf_op jit(solution)/shard_map/all_gather | solution.py:70
  172.6 15.3 %copy.13 = bf16[1,1664,3200]{2,1,0:T(8,128)(2,1)} copy(bf16[1,1664,3200]{2,0,1:T(2,128)(2,1)} %all-gather.3.cloned.1.call-done) | data formatting | bytes 21299200
  188.0 8.4 broadcast_in_dim.59
  196.5 443.6 %while.21 = (s32[]{:T(128)}, f32[1664,3200]{1,0:T(8,128)}, bf16[5,32,1664]{2,1,0:T(8,128)(2,1)S(1)}, bf16[32,3200]{1,0:T(8,128)(2,1)S(1)}, bf16[32,1664]{1,0:T(8...) while((s32[]{:T(128)}, f32[1664,3200]{1,0:T(8,128)}, ...), condition=%wide.region_13.14_spmd, body=%wide.region_0.13_spmd.sunk | while | flops 690257984 | bytes 59273832 | solution.py:135
  199.8 1.4 conditional.4
  203.5 32.2 %all-reduce.4.cloned.1.call-done = bf16[32,1664]{1,0:T(8,128)(2,1)} async-done(((bf16[32,1664]{1,0:T(8,128)(2,1)}), bf16[32,1664]{1,0:T(8,128)(2,1)}) %all-reduce.4.cloned.1.call-update) | async-done | bytes 106512 | tf_op jit(solution)/shard_map/while/body/eval_jaxpr/psum | solution.py:118
  239.2 5.7 collective-permute-done.1
  248.2 1.4 conditional.4
  251.8 47.5 %all-reduce.4.cloned.1.call-done = bf16[32,1664]{1,0:T(8,128)(2,1)} async-done(((bf16[32,1664]{1,0:T(8,128)(2,1)}), bf16[32,1664]{1,0:T(8,128)(2,1)}) %all-reduce.4.cloned.1.call-update) | async-done | bytes 106512 | tf_op jit(solution)/shard_map/while/body/eval_jaxpr/psum | solution.py:118
  302.8 5.7 collective-permute-done.1
  311.8 1.4 conditional.4
  315.4 49.2 %all-reduce.4.cloned.1.call-done = bf16[32,1664]{1,0:T(8,128)(2,1)} async-done(((bf16[32,1664]{1,0:T(8,128)(2,1)}), bf16[32,1664]{1,0:T(8,128)(2,1)}) %all-reduce.4.cloned.1.call-update) | async-done | bytes 106512 | tf_op jit(solution)/shard_map/while/body/eval_jaxpr/psum | solution.py:118
  368.1 5.7 collective-permute-done.1
  377.1 9.3 %conditional.4 = (bf16[32,1664]{1,0:T(8,128)(2,1)S(1)}, bf16[32,3200]{1,0:T(8,128)(2,1)S(1)}, bf16[32,1664]{1,0:T(8,128)(2,1)}, bf16[32,3200]{1,0:T(8,128)(2,1)}) conditional(s32[]{:T(128)} %clamp.6, () %tuple.65, (bf16[32,1664]{1,0:T(8,128)(2,1)S(1)}, f32[1,1664]{1,0:T(1,128)S(1)}, bf16[1664,3200]{1,0:T(8,128)(2,1)}, ...), branch_computations={%region_1.1_spmd, %region_2.2_spmd, %region_3.5_spmd} | conditional | flops 342601760 | bytes 12227238 | solution.py:110
  379.2 7.2 fusion.36
  388.7 41.3 %all-reduce.4.cloned.1.call-done = bf16[32,1664]{1,0:T(8,128)(2,1)} async-done(((bf16[32,1664]{1,0:T(8,128)(2,1)}), bf16[32,1664]{1,0:T(8,128)(2,1)}) %all-reduce.4.cloned.1.call-update) | async-done | bytes 106512 | tf_op jit(solution)/shard_map/while/body/eval_jaxpr/psum | solution.py:118
  433.5 17.3 %conditional.5 = (f32[1664,3200]{1,0:T(8,128)}) conditional(s32[]{:T(128)} %convert_element_type.179, f32[1664,3200]{1,0:T(8,128)} %get-tuple-element.404, (bf16[32,1664]{1,0:T(8,128)(2,1)}, bf16[32,3200]{1,0:T(8,128)(2,1)}, f32[1664,3200]{1,0:T(8,128)}) %tuple.68), branch_computations={%region_6.6_spmd, %region_7.7_spmd} | conditional | flops 346112000 | bytes 42909704 | solution.py:124
  433.5 17.3 %convolution_add_fusion = f32[1664,3200]{1,0:T(8,128)} fusion(f32[1664,3200]{1,0:T(8,128)} %get-tuple-element.188, bf16[32,1664]{1,0:T(8,128)(2,1)} %get-tuple-element.189, bf16[32,3200]{1,0:T(8,128)(2,1)} %get-tuple-element.190), kind=kOutput, calls=%fused_computation | convolution fusion | flops 346112000 | bytes 42909696 | tf_op jit(solution)/shard_map/while/body/eval_jaxpr/cond/branch_1_fun/dot_general | solution.py:52
  454.1 9.3 %conditional.4 = (bf16[32,1664]{1,0:T(8,128)(2,1)S(1)}, bf16[32,3200]{1,0:T(8,128)(2,1)S(1)}, bf16[32,1664]{1,0:T(8,128)(2,1)}, bf16[32,3200]{1,0:T(8,128)(2,1)}) conditional(s32[]{:T(128)} %clamp.6, () %tuple.65, (bf16[32,1664]{1,0:T(8,128)(2,1)S(1)}, f32[1,1664]{1,0:T(1,128)S(1)}, bf16[1664,3200]{1,0:T(8,128)(2,1)}, ...), branch_computations={%region_1.1_spmd, %region_2.2_spmd, %region_3.5_spmd} | conditional | flops 342601760 | bytes 12227238 | solution.py:110
  456.2 7.2 fusion.36
  465.7 29.7 %all-reduce.4.cloned.1.call-done = bf16[32,1664]{1,0:T(8,128)(2,1)} async-done(((bf16[32,1664]{1,0:T(8,128)(2,1)}), bf16[32,1664]{1,0:T(8,128)(2,1)}) %all-reduce.4.cloned.1.call-update) | async-done | bytes 106512 | tf_op jit(solution)/shard_map/while/body/eval_jaxpr/psum | solution.py:118
  498.9 17.3 %conditional.5 = (f32[1664,3200]{1,0:T(8,128)}) conditional(s32[]{:T(128)} %convert_element_type.179, f32[1664,3200]{1,0:T(8,128)} %get-tuple-element.404, (bf16[32,1664]{1,0:T(8,128)(2,1)}, bf16[32,3200]{1,0:T(8,128)(2,1)}, f32[1664,3200]{1,0:T(8,128)}) %tuple.68), branch_computations={%region_6.6_spmd, %region_7.7_spmd} | conditional | flops 346112000 | bytes 42909704 | solution.py:124
  498.9 17.3 %convolution_add_fusion = f32[1664,3200]{1,0:T(8,128)} fusion(f32[1664,3200]{1,0:T(8,128)} %get-tuple-element.188, bf16[32,1664]{1,0:T(8,128)(2,1)} %get-tuple-element.189, bf16[32,3200]{1,0:T(8,128)(2,1)} %get-tuple-element.190), kind=kOutput, calls=%fused_computation | convolution fusion | flops 346112000 | bytes 42909696 | tf_op jit(solution)/shard_map/while/body/eval_jaxpr/cond/branch_1_fun/dot_general | solution.py:52
  519.5 9.3 %conditional.4 = (bf16[32,1664]{1,0:T(8,128)(2,1)S(1)}, bf16[32,3200]{1,0:T(8,128)(2,1)S(1)}, bf16[32,1664]{1,0:T(8,128)(2,1)}, bf16[32,3200]{1,0:T(8,128)(2,1)}) conditional(s32[]{:T(128)} %clamp.6, () %tuple.65, (bf16[32,1664]{1,0:T(8,128)(2,1)S(1)}, f32[1,1664]{1,0:T(1,128)S(1)}, bf16[1664,3200]{1,0:T(8,128)(2,1)}, ...), branch_computations={%region_1.1_spmd, %region_2.2_spmd, %region_3.5_spmd} | conditional | flops 342601760 | bytes 12227238 | solution.py:110
  521.5 7.2 fusion.36
  531.1 26.4 %all-reduce.4.cloned.1.call-done = bf16[32,1664]{1,0:T(8,128)(2,1)} async-done(((bf16[32,1664]{1,0:T(8,128)(2,1)}), bf16[32,1664]{1,0:T(8,128)(2,1)}) %all-reduce.4.cloned.1.call-update) | async-done | bytes 106512 | tf_op jit(solution)/shard_map/while/body/eval_jaxpr/psum | solution.py:118
  561.0 17.3 %conditional.5 = (f32[1664,3200]{1,0:T(8,128)}) conditional(s32[]{:T(128)} %convert_element_type.179, f32[1664,3200]{1,0:T(8,128)} %get-tuple-element.404, (bf16[32,1664]{1,0:T(8,128)(2,1)}, bf16[32,3200]{1,0:T(8,128)(2,1)}, f32[1664,3200]{1,0:T(8,128)}) %tuple.68), branch_computations={%region_6.6_spmd, %region_7.7_spmd} | conditional | flops 346112000 | bytes 42909704 | solution.py:124
  561.0 17.3 %convolution_add_fusion = f32[1664,3200]{1,0:T(8,128)} fusion(f32[1664,3200]{1,0:T(8,128)} %get-tuple-element.188, bf16[32,1664]{1,0:T(8,128)(2,1)} %get-tuple-element.189, bf16[32,3200]{1,0:T(8,128)(2,1)} %get-tuple-element.190), kind=kOutput, calls=%fused_computation | convolution fusion | flops 346112000 | bytes 42909696 | tf_op jit(solution)/shard_map/while/body/eval_jaxpr/cond/branch_1_fun/dot_general | solution.py:52
  581.6 9.3 %conditional.4 = (bf16[32,1664]{1,0:T(8,128)(2,1)S(1)}, bf16[32,3200]{1,0:T(8,128)(2,1)S(1)}, bf16[32,1664]{1,0:T(8,128)(2,1)}, bf16[32,3200]{1,0:T(8,128)(2,1)}) conditional(s32[]{:T(128)} %clamp.6, () %tuple.65, (bf16[32,1664]{1,0:T(8,128)(2,1)S(1)}, f32[1,1664]{1,0:T(1,128)S(1)}, bf16[1664,3200]{1,0:T(8,128)(2,1)}, ...), branch_computations={%region_1.1_spmd, %region_2.2_spmd, %region_3.5_spmd} | conditional | flops 342601760 | bytes 12227238 | solution.py:110
  583.6 7.2 fusion.36
  593.1 26.1 %all-reduce.4.cloned.1.call-done = bf16[32,1664]{1,0:T(8,128)(2,1)} async-done(((bf16[32,1664]{1,0:T(8,128)(2,1)}), bf16[32,1664]{1,0:T(8,128)(2,1)}) %all-reduce.4.cloned.1.call-update) | async-done | bytes 106512 | tf_op jit(solution)/shard_map/while/body/eval_jaxpr/psum | solution.py:118
  622.7 17.3 %conditional.5 = (f32[1664,3200]{1,0:T(8,128)}) conditional(s32[]{:T(128)} %convert_element_type.179, f32[1664,3200]{1,0:T(8,128)} %get-tuple-element.404, (bf16[32,1664]{1,0:T(8,128)(2,1)}, bf16[32,3200]{1,0:T(8,128)(2,1)}, f32[1664,3200]{1,0:T(8,128)}) %tuple.68), branch_computations={%region_6.6_spmd, %region_7.7_spmd} | conditional | flops 346112000 | bytes 42909704 | solution.py:124
  622.8 17.3 %convolution_add_fusion = f32[1664,3200]{1,0:T(8,128)} fusion(f32[1664,3200]{1,0:T(8,128)} %get-tuple-element.188, bf16[32,1664]{1,0:T(8,128)(2,1)} %get-tuple-element.189, bf16[32,3200]{1,0:T(8,128)(2,1)} %get-tuple-element.190), kind=kOutput, calls=%fused_computation | convolution fusion | flops 346112000 | bytes 42909696 | tf_op jit(solution)/shard_map/while/body/eval_jaxpr/cond/branch_1_fun/dot_general | solution.py:52
  640.1 12.3 %convert_element_type.68 = bf16[1664,3200]{1,0:T(8,128)(2,1)} convert(f32[1664,3200]{1,0:T(8,128)} %get-tuple-element.215) | non-fusion elementwise | flops 5324800 | bytes 31948800 | tf_op jit(solution)/shard_map/convert_element_type | solution.py:138
  652.4 150.3 %fusion = bf16[64,3200]{1,0:T(8,128)(2,1)S(1)} fusion(bf16[1664,3200]{1,0:T(8,128)(2,1)} %convert_element_type.68), kind=kCustom, calls=%all-reduce-scatter | all-reduce-scatter fusion | flops 6553601 | bytes 11060224
  802.8 2.0 collective-permute-start.7
  806.0 1.9 collective-permute-start.2
  807.9 5.7 collective-permute-start.3
  813.7 1.9 collective-permute-start.4
  815.6 1.9 collective-permute-start.5
  817.5 11.5 %collective-permute-done.7 = bf16[52,3200]{1,0:T(8,128)(2,1)S(1)} collective-permute-done((bf16[52,3200]{1,0:T(8,128)(2,1)S(1)}, bf16[52,3200]{1,0:T(8,128)(2,1)S(1)}, u32[]{:S(2)}, u32[]{:S(2)}) %collective-permute-start.7) | collective-permute-done | bytes 332832
  829.0 1.9 collective-permute-start.6
  831.7 7.9 collective-permute-done.2
  839.6 1.4 collective-permute-done.3
  842.7 46.2 %collective-permute-done.6 = bf16[64,3200]{1,0:T(8,128)(2,1)} collective-permute-done((bf16[64,3200]{1,0:T(8,128)(2,1)S(1)}, bf16[64,3200]{1,0:T(8,128)(2,1)}, u32[]{:S(2)}, u32[]{:S(2)}) %collective-permute-start.6) | collective-permute-done | bytes 409632
  888.8 21.1 %concatenate = bf16[436,3200]{1,0:T(8,128)(2,1)S(1)} concatenate(bf16[52,3200]{1,0:T(8,128)(2,1)} %copy-done.6, bf16[64,3200]{1,0:T(8,128)(2,1)} %collective-permute-done.6, bf16[64,3200]{1,0:T(8,128)(2,1)} %copy-done.5, bf16[64,3200]{1,0:T(8,128)(2,1)} %copy-done.4, bf16[64,3200]{1,0:T(8,128)(2,1)} %copy-done.3, bf16[64,3200]{1,0:T(8,128)(2,1)} %copy-done.2, ...), dimensions={0} | concatenate | bytes 5580800
  (204 shorter events, 75.0 us)
Async XLA Ops:
  7.2 165.5 %all-gather.3.cloned.1.call-start = ((), (), s32[]{:S(2)}) async-start(), calls=%async_computation | async-start | bytes 21964800 | tf_op jit(solution)/shard_map/all_gather | solution.py:70
  188.0 8.5 copy-start.1
  196.5 39.1 %all-reduce.4.cloned.1.call-start = ((), (), s32[]{:S(2)}) async-start(), calls=%async_computation.1 | async-start | bytes 212992 | tf_op jit(solution)/shard_map/while/body/eval_jaxpr/psum | solution.py:118
  201.2 0.7 copy-start
  201.9 37.2 %collective-permute-start = (bf16[32,3200]{1,0:T(8,128)(2,1)S(1)}, bf16[32,3200]{1,0:T(8,128)(2,1)S(1)}, u32[]{:S(2)}, u32[]{:S(2)}) collective-permute-start(bf16[32,3200]{1,0:T(8,128)(2,1)S(1)} %get-tuple-element.368), channel_id=1, source_target_pairs={{64,0},{128,64},{192,128},{65,1},{129,65},{193,129},{66,2},{130,66... | collective-permute-start | bytes 614408 | tf_op jit(solution)/shard_map/while/body/eval_jaxpr/ppermute | solution.py:22
  237.8 7.1 collective-permute-start.1
  244.9 54.4 %all-reduce.4.cloned.1.call-start = ((), (), s32[]{:S(2)}) async-start(), calls=%async_computation.1 | async-start | bytes 212992 | tf_op jit(solution)/shard_map/while/body/eval_jaxpr/psum | solution.py:118
  249.6 0.7 copy-start
  250.2 52.5 %collective-permute-start = (bf16[32,3200]{1,0:T(8,128)(2,1)S(1)}, bf16[32,3200]{1,0:T(8,128)(2,1)S(1)}, u32[]{:S(2)}, u32[]{:S(2)}) collective-permute-start(bf16[32,3200]{1,0:T(8,128)(2,1)S(1)} %get-tuple-element.368), channel_id=1, source_target_pairs={{64,0},{128,64},{192,128},{65,1},{129,65},{193,129},{66,2},{130,66... | collective-permute-start | bytes 614408 | tf_op jit(solution)/shard_map/while/body/eval_jaxpr/ppermute | solution.py:22
  301.4 7.1 collective-permute-start.1
  308.5 56.1 %all-reduce.4.cloned.1.call-start = ((), (), s32[]{:S(2)}) async-start(), calls=%async_computation.1 | async-start | bytes 212992 | tf_op jit(solution)/shard_map/while/body/eval_jaxpr/psum | solution.py:118
  313.2 0.7 copy-start
  313.9 54.3 %collective-permute-start = (bf16[32,3200]{1,0:T(8,128)(2,1)S(1)}, bf16[32,3200]{1,0:T(8,128)(2,1)S(1)}, u32[]{:S(2)}, u32[]{:S(2)}) collective-permute-start(bf16[32,3200]{1,0:T(8,128)(2,1)S(1)} %get-tuple-element.368), channel_id=1, source_target_pairs={{64,0},{128,64},{192,128},{65,1},{129,65},{193,129},{66,2},{130,66... | collective-permute-start | bytes 614408 | tf_op jit(solution)/shard_map/while/body/eval_jaxpr/ppermute | solution.py:22
  366.8 7.1 collective-permute-start.1
  373.9 56.1 %all-reduce.4.cloned.1.call-start = ((), (), s32[]{:S(2)}) async-start(), calls=%async_computation.1 | async-start | bytes 212992 | tf_op jit(solution)/shard_map/while/body/eval_jaxpr/psum | solution.py:118
  386.5 0.7 copy-start
  387.2 63.6 %collective-permute-start = (bf16[32,3200]{1,0:T(8,128)(2,1)S(1)}, bf16[32,3200]{1,0:T(8,128)(2,1)S(1)}, u32[]{:S(2)}, u32[]{:S(2)}) collective-permute-start(bf16[32,3200]{1,0:T(8,128)(2,1)S(1)} %get-tuple-element.368), channel_id=1, source_target_pairs={{64,0},{128,64},{192,128},{65,1},{129,65},{193,129},{66,2},{130,66... | collective-permute-start | bytes 614408 | tf_op jit(solution)/shard_map/while/body/eval_jaxpr/ppermute | solution.py:22
  432.2 18.6 %collective-permute-start.1 = (bf16[32,1664]{1,0:T(8,128)(2,1)S(1)}, bf16[32,1664]{1,0:T(8,128)(2,1)S(1)}, u32[]{:S(2)}, u32[]{:S(2)}) collective-permute-start(bf16[32,1664]{1,0:T(8,128)(2,1)S(1)} %get-tuple-element.369), channel_id=1, source_target_pairs={{64,0},{128,64},{192,128},{65,1},{129,65},{193,129},{66,2},{130,66... | collective-permute-start | bytes 319496 | tf_op jit(solution)/shard_map/while/body/eval_jaxpr/ppermute | solution.py:22
  450.8 44.6 %all-reduce.4.cloned.1.call-start = ((), (), s32[]{:S(2)}) async-start(), calls=%async_computation.1 | async-start | bytes 212992 | tf_op jit(solution)/shard_map/while/body/eval_jaxpr/psum | solution.py:118
  463.5 0.7 copy-start
  464.1 52.1 %collective-permute-start = (bf16[32,3200]{1,0:T(8,128)(2,1)S(1)}, bf16[32,3200]{1,0:T(8,128)(2,1)S(1)}, u32[]{:S(2)}, u32[]{:S(2)}) collective-permute-start(bf16[32,3200]{1,0:T(8,128)(2,1)S(1)} %get-tuple-element.368), channel_id=1, source_target_pairs={{64,0},{128,64},{192,128},{65,1},{129,65},{193,129},{66,2},{130,66... | collective-permute-start | bytes 614408 | tf_op jit(solution)/shard_map/while/body/eval_jaxpr/ppermute | solution.py:22
  497.6 18.6 %collective-permute-start.1 = (bf16[32,1664]{1,0:T(8,128)(2,1)S(1)}, bf16[32,1664]{1,0:T(8,128)(2,1)S(1)}, u32[]{:S(2)}, u32[]{:S(2)}) collective-permute-start(bf16[32,1664]{1,0:T(8,128)(2,1)S(1)} %get-tuple-element.369), channel_id=1, source_target_pairs={{64,0},{128,64},{192,128},{65,1},{129,65},{193,129},{66,2},{130,66... | collective-permute-start | bytes 319496 | tf_op jit(solution)/shard_map/while/body/eval_jaxpr/ppermute | solution.py:22
  516.2 41.3 %all-reduce.4.cloned.1.call-start = ((), (), s32[]{:S(2)}) async-start(), calls=%async_computation.1 | async-start | bytes 212992 | tf_op jit(solution)/shard_map/while/body/eval_jaxpr/psum | solution.py:118
  528.8 0.7 copy-start
  529.5 48.7 %collective-permute-start = (bf16[32,3200]{1,0:T(8,128)(2,1)S(1)}, bf16[32,3200]{1,0:T(8,128)(2,1)S(1)}, u32[]{:S(2)}, u32[]{:S(2)}) collective-permute-start(bf16[32,3200]{1,0:T(8,128)(2,1)S(1)} %get-tuple-element.368), channel_id=1, source_target_pairs={{64,0},{128,64},{192,128},{65,1},{129,65},{193,129},{66,2},{130,66... | collective-permute-start | bytes 614408 | tf_op jit(solution)/shard_map/while/body/eval_jaxpr/ppermute | solution.py:22
  559.7 18.6 %collective-permute-start.1 = (bf16[32,1664]{1,0:T(8,128)(2,1)S(1)}, bf16[32,1664]{1,0:T(8,128)(2,1)S(1)}, u32[]{:S(2)}, u32[]{:S(2)}) collective-permute-start(bf16[32,1664]{1,0:T(8,128)(2,1)S(1)} %get-tuple-element.369), channel_id=1, source_target_pairs={{64,0},{128,64},{192,128},{65,1},{129,65},{193,129},{66,2},{130,66... | collective-permute-start | bytes 319496 | tf_op jit(solution)/shard_map/while/body/eval_jaxpr/ppermute | solution.py:22
  578.3 41.0 %all-reduce.4.cloned.1.call-start = ((), (), s32[]{:S(2)}) async-start(), calls=%async_computation.1 | async-start | bytes 212992 | tf_op jit(solution)/shard_map/while/body/eval_jaxpr/psum | solution.py:118
  590.9 0.7 copy-start
  591.6 48.5 %collective-permute-start = (bf16[32,3200]{1,0:T(8,128)(2,1)S(1)}, bf16[32,3200]{1,0:T(8,128)(2,1)S(1)}, u32[]{:S(2)}, u32[]{:S(2)}) collective-permute-start(bf16[32,3200]{1,0:T(8,128)(2,1)S(1)} %get-tuple-element.368), channel_id=1, source_target_pairs={{64,0},{128,64},{192,128},{65,1},{129,65},{193,129},{66,2},{130,66... | collective-permute-start | bytes 614408 | tf_op jit(solution)/shard_map/while/body/eval_jaxpr/ppermute | solution.py:22
  621.4 18.6 %collective-permute-start.1 = (bf16[32,1664]{1,0:T(8,128)(2,1)S(1)}, bf16[32,1664]{1,0:T(8,128)(2,1)S(1)}, u32[]{:S(2)}, u32[]{:S(2)}) collective-permute-start(bf16[32,1664]{1,0:T(8,128)(2,1)S(1)} %get-tuple-element.369), channel_id=1, source_target_pairs={{64,0},{128,64},{192,128},{65,1},{129,65},{193,129},{66,2},{130,66... | collective-permute-start | bytes 319496 | tf_op jit(solution)/shard_map/while/body/eval_jaxpr/ppermute | solution.py:22
  640.1 164.7 %copy-start.7 = (u32[256]{0:T(256)S(1)}, u32[256]{0:T(256)}, u32[]{:S(2)}) copy-start(u32[256]{0:T(256)} %constant.123) | copy-start | bytes 3076
  802.8 26.2 %collective-permute-start.7 = (bf16[52,3200]{1,0:T(8,128)(2,1)S(1)}, bf16[52,3200]{1,0:T(8,128)(2,1)S(1)}, u32[]{:S(2)}, u32[]{:S(2)}) collective-permute-start(bf16[52,3200]{1,0:T(8,128)(2,1)S(1)} %slice.4), channel_id=1, source_target_pairs={{0,12},{2,14},{4,16},{6,18},{8,20},{10,22},{12,24},{14,26},{16,28}... | collective-permute-start | bytes 998408
  806.0 33.6 %collective-permute-start.2 = (bf16[64,3200]{1,0:T(8,128)(2,1)S(1)}, bf16[64,3200]{1,0:T(8,128)(2,1)S(1)}, u32[]{:S(2)}, u32[]{:S(2)}) collective-permute-start(bf16[64,3200]{1,0:T(8,128)(2,1)S(1)} %fusion), channel_id=1, source_target_pairs={{0,2},{2,4},{4,6},{6,8},{8,10},{10,12},{12,14},{14,16},{16,18},{18... | collective-permute-start | bytes 1228808
  807.9 33.1 %collective-permute-start.3 = (bf16[64,3200]{1,0:T(8,128)(2,1)S(1)}, bf16[64,3200]{1,0:T(8,128)(2,1)S(1)}, u32[]{:S(2)}, u32[]{:S(2)}) collective-permute-start(bf16[64,3200]{1,0:T(8,128)(2,1)S(1)} %fusion), channel_id=1, source_target_pairs={{0,4},{2,6},{4,8},{6,10},{8,12},{10,14},{12,16},{14,18},{16,20},{1... | collective-permute-start | bytes 1228808
  813.7 27.3 %collective-permute-start.4 = (bf16[64,3200]{1,0:T(8,128)(2,1)S(1)}, bf16[64,3200]{1,0:T(8,128)(2,1)S(1)}, u32[]{:S(2)}, u32[]{:S(2)}) collective-permute-start(bf16[64,3200]{1,0:T(8,128)(2,1)S(1)} %fusion), channel_id=1, source_target_pairs={{0,6},{2,8},{4,10},{6,12},{8,14},{10,16},{12,18},{14,20},{16,22},{... | collective-permute-start | bytes 1228808
  815.6 25.4 %collective-permute-start.5 = (bf16[64,3200]{1,0:T(8,128)(2,1)S(1)}, bf16[64,3200]{1,0:T(8,128)(2,1)S(1)}, u32[]{:S(2)}, u32[]{:S(2)}) collective-permute-start(bf16[64,3200]{1,0:T(8,128)(2,1)S(1)} %fusion), channel_id=1, source_target_pairs={{0,8},{2,10},{4,12},{6,14},{8,16},{10,18},{12,20},{14,22},{16,24},... | collective-permute-start | bytes 1228808
  829.0 12.0 %copy-start.6 = (bf16[52,3200]{1,0:T(8,128)(2,1)}, bf16[52,3200]{1,0:T(8,128)(2,1)S(1)}, u32[]{:S(2)}) copy-start(bf16[52,3200]{1,0:T(8,128)(2,1)S(1)} %collective-permute-done.7) | copy-start | bytes 998404
  829.0 59.8 %collective-permute-start.6 = (bf16[64,3200]{1,0:T(8,128)(2,1)S(1)}, bf16[64,3200]{1,0:T(8,128)(2,1)}, u32[]{:S(2)}, u32[]{:S(2)}) collective-permute-start(bf16[64,3200]{1,0:T(8,128)(2,1)S(1)} %fusion), channel_id=1, source_target_pairs={{0,10},{2,12},{4,14},{6,16},{8,18},{10,20},{12,22},{14,24},{16,26}... | collective-permute-start | bytes 1228808
  839.6 1.4 copy-start.2
  841.0 0.8 copy-start.3
  841.0 0.9 copy-start.4
  841.9 0.7 copy-start.5
Sparse Core Ops, SparseCore 0:
  10.6 161.9 all-gather.2
  202.0 33.5 all-reduce.3
  250.4 48.8 all-reduce.3
  314.0 50.5 all-reduce.3
  387.3 42.6 all-reduce.3
  464.3 31.0 all-reduce.3
  529.6 27.7 all-reduce.3
  591.7 27.4 all-reduce.3
where the time goes:
time: 920 us; the launch traced here: 918 us
  waiting for transfers between devices  498 us (54%)
  blocking collectives  150 us (16%)
  matrix products  99.5 us (11%)
  local copies, waits for them, and re-layouts  70.8 us (8%)
  other arithmetic  45.2 us (5%)
  starting transfers between devices  33.6 us (4%)
  between operations  14.8 us (2%)
    psum x7, waiting for transfers between devices, advance(): lax.psum(shortened(partial_value), 'tensor')  252 us
    all_gather x1, waiting for transfers between devices, body(): full_weight = lax.all_gather(weights[0], 'dp', axis=0, tiled=True)  161 us
    unnamed x1, blocking collectives  150 us
    dot_general x4, matrix products, add_term(): lax.dot_general(left_side, right_side, (((0,), (0,)), ((), ())), preferre...  69.1 us
    unnamed x7, waiting for transfers between devices  66.9 us
    unnamed x19, local copies, waits for them, and re-layouts  41.1 us
    dot_general x4, matrix products, up_work(): lax.dot_general(act_grad, full_weight, (((1,), (1,)), ((), ())), preferre...  29 us
  transfers between devices with their start and end apart: 28, of which 15 were waited for; matrix products, arithmetic and copies ran while one was open for 10% of the time, Pallas kernels for 0%

commit v1 on v0

--- a/solution.py
+++ b/solution.py
@@ -115,7 +115,8 @@
         inv_std = lax.rsqrt(jnp.mean(center * center, axis=-1, keepdims=True) + norm_eps)
         unit_rows = center * inv_std
         summed = jax.tree.map(
-            lambda part: part.astype(jnp.float32), lax.psum(shortened(partial_value), "tensor")
+            lambda part: part.astype(jnp.float32),
+            jnp.sum(lax.all_gather(shortened(partial_value), "tensor"), axis=0),
         )
         back_out = norm_back(incoming, summed, unit_rows, inv_std, channel_gain)
         outgoing = jnp.where(is_up, back_out, incoming)

time: 920 us -> 687 us (0.75)
  waiting for transfers between devices: 498 us -> 261 us
  other arithmetic: 45.2 us -> 33 us
  blocking collectives: 150 us -> 162 us
    psum x7 -> x0, waiting for transfers between devices: 252 us -> none  [advance(): lax.psum(shortened(partial_value), 'tensor')]
    ppermute x14, waiting for transfers between devices: 17.2 us -> 40.4 us  [shifted(): return lax.ppermute(block, axis, route)]
    all_gather x0 -> x7, blocking collectives: none -> 13.7 us  [advance(): lax.all_gather(shortened(partial_value), 'tensor')]
  transfers between devices with their start and end apart: 28 -> 21, of which waited for: 15 -> 10; matrix products, arithmetic and copies ran while one was open for 10% -> 11% of each run, Pallas kernels for 0% -> 0%
where the time goes in v1:
time: 687 us; the launch traced here: 676 us
  waiting for transfers between devices  261 us (38%)
  blocking collectives  162 us (24%)
  matrix products  99.4 us (14%)
  local copies, waits for them, and re-layouts  66.4 us (10%)
  starting transfers between devices  34.2 us (5%)
  other arithmetic  33 us (5%)
  between operations  14.9 us (2%)
    all_gather x1, waiting for transfers between devices, body(): full_weight = lax.all_gather(weights[0], 'dp', axis=0, tiled=True)  161 us
    unnamed x1, blocking collectives  148 us
    dot_general x4, matrix products, add_term(): lax.dot_general(left_side, right_side, (((0,), (0,)), ((), ())), preferre...  69.1 us
    unnamed x7, waiting for transfers between devices  59.4 us
    unnamed x19, local copies, waits for them, and re-layouts  41.2 us
    ppermute x14, waiting for transfers between devices, shifted(): return lax.ppermute(block, axis, route)  40.4 us
    dot_general x4, matrix products, up_work(): lax.dot_general(act_grad, full_weight, (((1,), (1,)), ((), ())), preferre...  29 us
    ppermute x14, starting transfers between devices, shifted(): return lax.ppermute(block, axis, route)  18 us
  transfers between devices with their start and end apart: 21, of which 10 were waited for; matrix products, arithmetic and copies ran while one was open for 11% of the time, Pallas kernels for 0%

profile of v1, /device:TPU:160, one launch (start us, length us, event | category | flops | bytes accessed | tf_op | source)
XLA Modules:
  0.0 676.4 jit_solution(649955820540310940)
XLA Ops:
  7.2 2.4 copy.10
  10.3 1.4 convolution_convert_fusion.1
  11.7 160.9 %all-gather.6.cloned.1.call-done = bf16[1,1664,3200]{2,0,1:T(2,128)(2,1)} async-done(((bf16[1,52,3200]{2,0,1:T(2,128)(2,1)}), bf16[1,1664,3200]{2,0,1:T(2,128)(2,1)}) %all-gather.6.cloned.1.call-update) | async-done | bytes 10649616 | tf_op jit(solution)/shard_map/all_gather | solution.py:70
  172.6 15.3 %copy.13 = bf16[1,1664,3200]{2,1,0:T(8,128)(2,1)} copy(bf16[1,1664,3200]{2,0,1:T(2,128)(2,1)} %all-gather.6.cloned.1.call-done) | data formatting | bytes 21299200
  188.0 8.4 %broadcast_in_dim.60 = f32[1664,3200]{1,0:T(8,128)} broadcast(f32[]{:T(128)} %constant.119.clone.1), dimensions={} | broadcast | bytes 21299204 | tf_op jit(solution)/shard_map/broadcast_in_dim | solution.py:132
  196.5 210.8 %while.21 = (s32[]{:T(128)}, f32[1664,3200]{1,0:T(8,128)}, bf16[5,32,1664]{2,1,0:T(8,128)(2,1)S(1)}, bf16[32,3200]{1,0:T(8,128)(2,1)S(1)}, bf16[32,1664]{1,0:T(8...) while((s32[]{:T(128)}, f32[1664,3200]{1,0:T(8,128)}, ...), condition=%wide.region_13.14_spmd, body=%wide.region_0.13_spmd.sunk | while | flops 690257984 | bytes 58847792 | solution.py:136
  199.8 1.4 conditional.4
  202.5 2.0 all-gather.3
  206.4 6.5 collective-permute-done.1
  216.2 1.4 conditional.4
  218.9 2.0 all-gather.3
  222.9 6.5 collective-permute-done.1
  232.7 1.4 conditional.4
  235.3 2.0 all-gather.3
  239.3 23.6 %collective-permute-done.1 = bf16[32,1664]{1,0:T(8,128)(2,1)S(1)} collective-permute-done((bf16[32,1664]{1,0:T(8,128)(2,1)S(1)}, bf16[32,1664]{1,0:T(8,128)(2,1)S(1)}, u32[]{:S(2)}, u32[]{:S(2)}) %collective-permute-start.1) | collective-permute-done | bytes 106528 | tf_op jit(solution)/shard_map/while/body/eval_jaxpr/ppermute | solution.py:22
  266.2 9.3 %conditional.4 = (bf16[32,1664]{1,0:T(8,128)(2,1)S(1)}, bf16[32,3200]{1,0:T(8,128)(2,1)S(1)}, bf16[32,1664]{1,0:T(8,128)(2,1)}, bf16[32,3200]{1,0:T(8,128)(2,1)}) conditional(s32[]{:T(128)} %clamp.7, () %tuple.67, (bf16[32,1664]{1,0:T(8,128)(2,1)S(1)}, f32[1,1664]{1,0:T(1,128)S(1)}, bf16[1664,3200]{1,0:T(8,128)(2,1)}, ...), branch_computations={%region_1.1_spmd, %region_2.2_spmd, %region_3.5_spmd} | conditional | flops 342601760 | bytes 12227238 | solution.py:110
  268.2 7.2 %fusion.36 = bf16[32,1664]{1,0:T(8,128)(2,1)S(1)} fusion(bf16[32,3200]{1,0:T(8,128)(2,1)} %fusion.12, bf16[1664,3200]{1,0:T(8,128)(2,1)} %get-tuple-element.201), kind=kOutput, calls=%fused_computation.64 | convolution fusion | flops 340787200 | bytes 10960896 | tf_op jit(solution)/shard_map/while/body/eval_jaxpr/cond/branch_2_fun/dot_general | solution.py:96
  275.5 1.3 collective-permute-start
  276.8 2.0 all-gather.3
  280.8 17.3 %conditional.5 = (f32[1664,3200]{1,0:T(8,128)}) conditional(s32[]{:T(128)} %convert_element_type.187, f32[1664,3200]{1,0:T(8,128)} %get-tuple-element.421, (bf16[32,1664]{1,0:T(8,128)(2,1)}, bf16[32,3200]{1,0:T(8,128)(2,1)}, f32[1664,3200]{1,0:T(8,128)}) %tuple.70), branch_computations={%region_6.6_spmd, %region_7.7_spmd} | conditional | flops 346112000 | bytes 42909704 | solution.py:125
  280.8 17.3 %convolution_add_fusion = f32[1664,3200]{1,0:T(8,128)} fusion(f32[1664,3200]{1,0:T(8,128)} %get-tuple-element.204, bf16[32,1664]{1,0:T(8,128)(2,1)} %get-tuple-element.205, bf16[32,3200]{1,0:T(8,128)(2,1)} %get-tuple-element.206), kind=kOutput, calls=%fused_computation | convolution fusion | flops 346112000 | bytes 42909696 | tf_op jit(solution)/shard_map/while/body/eval_jaxpr/cond/branch_1_fun/dot_general | solution.py:52
  302.6 9.3 %conditional.4 = (bf16[32,1664]{1,0:T(8,128)(2,1)S(1)}, bf16[32,3200]{1,0:T(8,128)(2,1)S(1)}, bf16[32,1664]{1,0:T(8,128)(2,1)}, bf16[32,3200]{1,0:T(8,128)(2,1)}) conditional(s32[]{:T(128)} %clamp.7, () %tuple.67, (bf16[32,1664]{1,0:T(8,128)(2,1)S(1)}, f32[1,1664]{1,0:T(1,128)S(1)}, bf16[1664,3200]{1,0:T(8,128)(2,1)}, ...), branch_computations={%region_1.1_spmd, %region_2.2_spmd, %region_3.5_spmd} | conditional | flops 342601760 | bytes 12227238 | solution.py:110
  304.7 7.2 %fusion.36 = bf16[32,1664]{1,0:T(8,128)(2,1)S(1)} fusion(bf16[32,3200]{1,0:T(8,128)(2,1)} %fusion.12, bf16[1664,3200]{1,0:T(8,128)(2,1)} %get-tuple-element.201), kind=kOutput, calls=%fused_computation.64 | convolution fusion | flops 340787200 | bytes 10960896 | tf_op jit(solution)/shard_map/while/body/eval_jaxpr/cond/branch_2_fun/dot_general | solution.py:96
  313.3 2.0 all-gather.3
  317.2 17.3 %conditional.5 = (f32[1664,3200]{1,0:T(8,128)}) conditional(s32[]{:T(128)} %convert_element_type.187, f32[1664,3200]{1,0:T(8,128)} %get-tuple-element.421, (bf16[32,1664]{1,0:T(8,128)(2,1)}, bf16[32,3200]{1,0:T(8,128)(2,1)}, f32[1664,3200]{1,0:T(8,128)}) %tuple.70), branch_computations={%region_6.6_spmd, %region_7.7_spmd} | conditional | flops 346112000 | bytes 42909704 | solution.py:125
  317.2 17.3 %convolution_add_fusion = f32[1664,3200]{1,0:T(8,128)} fusion(f32[1664,3200]{1,0:T(8,128)} %get-tuple-element.204, bf16[32,1664]{1,0:T(8,128)(2,1)} %get-tuple-element.205, bf16[32,3200]{1,0:T(8,128)(2,1)} %get-tuple-element.206), kind=kOutput, calls=%fused_computation | convolution fusion | flops 346112000 | bytes 42909696 | tf_op jit(solution)/shard_map/while/body/eval_jaxpr/cond/branch_1_fun/dot_general | solution.py:52
  339.0 9.3 %conditional.4 = (bf16[32,1664]{1,0:T(8,128)(2,1)S(1)}, bf16[32,3200]{1,0:T(8,128)(2,1)S(1)}, bf16[32,1664]{1,0:T(8,128)(2,1)}, bf16[32,3200]{1,0:T(8,128)(2,1)}) conditional(s32[]{:T(128)} %clamp.7, () %tuple.67, (bf16[32,1664]{1,0:T(8,128)(2,1)S(1)}, f32[1,1664]{1,0:T(1,128)S(1)}, bf16[1664,3200]{1,0:T(8,128)(2,1)}, ...), branch_computations={%region_1.1_spmd, %region_2.2_spmd, %region_3.5_spmd} | conditional | flops 342601760 | bytes 12227238 | solution.py:110
  341.1 7.2 %fusion.36 = bf16[32,1664]{1,0:T(8,128)(2,1)S(1)} fusion(bf16[32,3200]{1,0:T(8,128)(2,1)} %fusion.12, bf16[1664,3200]{1,0:T(8,128)(2,1)} %get-tuple-element.201), kind=kOutput, calls=%fused_computation.64 | convolution fusion | flops 340787200 | bytes 10960896 | tf_op jit(solution)/shard_map/while/body/eval_jaxpr/cond/branch_2_fun/dot_general | solution.py:96
  349.7 2.0 all-gather.3
  353.6 17.3 %conditional.5 = (f32[1664,3200]{1,0:T(8,128)}) conditional(s32[]{:T(128)} %convert_element_type.187, f32[1664,3200]{1,0:T(8,128)} %get-tuple-element.421, (bf16[32,1664]{1,0:T(8,128)(2,1)}, bf16[32,3200]{1,0:T(8,128)(2,1)}, f32[1664,3200]{1,0:T(8,128)}) %tuple.70), branch_computations={%region_6.6_spmd, %region_7.7_spmd} | conditional | flops 346112000 | bytes 42909704 | solution.py:125
  353.6 17.3 %convolution_add_fusion = f32[1664,3200]{1,0:T(8,128)} fusion(f32[1664,3200]{1,0:T(8,128)} %get-tuple-element.204, bf16[32,1664]{1,0:T(8,128)(2,1)} %get-tuple-element.205, bf16[32,3200]{1,0:T(8,128)(2,1)} %get-tuple-element.206), kind=kOutput, calls=%fused_computation | convolution fusion | flops 346112000 | bytes 42909696 | tf_op jit(solution)/shard_map/while/body/eval_jaxpr/cond/branch_1_fun/dot_general | solution.py:52
  375.4 9.3 %conditional.4 = (bf16[32,1664]{1,0:T(8,128)(2,1)S(1)}, bf16[32,3200]{1,0:T(8,128)(2,1)S(1)}, bf16[32,1664]{1,0:T(8,128)(2,1)}, bf16[32,3200]{1,0:T(8,128)(2,1)}) conditional(s32[]{:T(128)} %clamp.7, () %tuple.67, (bf16[32,1664]{1,0:T(8,128)(2,1)S(1)}, f32[1,1664]{1,0:T(1,128)S(1)}, bf16[1664,3200]{1,0:T(8,128)(2,1)}, ...), branch_computations={%region_1.1_spmd, %region_2.2_spmd, %region_3.5_spmd} | conditional | flops 342601760 | bytes 12227238 | solution.py:110
  377.5 7.2 %fusion.36 = bf16[32,1664]{1,0:T(8,128)(2,1)S(1)} fusion(bf16[32,3200]{1,0:T(8,128)(2,1)} %fusion.12, bf16[1664,3200]{1,0:T(8,128)(2,1)} %get-tuple-element.201), kind=kOutput, calls=%fused_computation.64 | convolution fusion | flops 340787200 | bytes 10960896 | tf_op jit(solution)/shard_map/while/body/eval_jaxpr/cond/branch_2_fun/dot_general | solution.py:96
  386.1 2.0 all-gather.3
  390.0 17.3 %conditional.5 = (f32[1664,3200]{1,0:T(8,128)}) conditional(s32[]{:T(128)} %convert_element_type.187, f32[1664,3200]{1,0:T(8,128)} %get-tuple-element.421, (bf16[32,1664]{1,0:T(8,128)(2,1)}, bf16[32,3200]{1,0:T(8,128)(2,1)}, f32[1664,3200]{1,0:T(8,128)}) %tuple.70), branch_computations={%region_6.6_spmd, %region_7.7_spmd} | conditional | flops 346112000 | bytes 42909704 | solution.py:125
  390.0 17.3 %convolution_add_fusion = f32[1664,3200]{1,0:T(8,128)} fusion(f32[1664,3200]{1,0:T(8,128)} %get-tuple-element.204, bf16[32,1664]{1,0:T(8,128)(2,1)} %get-tuple-element.205, bf16[32,3200]{1,0:T(8,128)(2,1)} %get-tuple-element.206), kind=kOutput, calls=%fused_computation | convolution fusion | flops 346112000 | bytes 42909696 | tf_op jit(solution)/shard_map/while/body/eval_jaxpr/cond/branch_1_fun/dot_general | solution.py:52
  407.3 12.3 %convert_element_type.76 = bf16[1664,3200]{1,0:T(8,128)(2,1)} convert(f32[1664,3200]{1,0:T(8,128)} %get-tuple-element.231) | non-fusion elementwise | flops 5324800 | bytes 31948800 | tf_op jit(solution)/shard_map/convert_element_type | solution.py:139
  419.7 148.4 %fusion = bf16[64,3200]{1,0:T(8,128)(2,1)S(1)} fusion(bf16[1664,3200]{1,0:T(8,128)(2,1)} %convert_element_type.76), kind=kCustom, calls=%all-reduce-scatter | all-reduce-scatter fusion | flops 6553601 | bytes 11060224
  568.2 2.7 collective-permute-start.7
  572.1 1.9 collective-permute-start.2
  574.1 5.8 collective-permute-start.3
  579.9 1.9 collective-permute-start.4
  581.8 1.9 collective-permute-start.5
  583.7 8.7 %collective-permute-done.7 = bf16[52,3200]{1,0:T(8,128)(2,1)S(1)} collective-permute-done((bf16[52,3200]{1,0:T(8,128)(2,1)S(1)}, bf16[52,3200]{1,0:T(8,128)(2,1)S(1)}, u32[]{:S(2)}, u32[]{:S(2)}) %collective-permute-start.7) | collective-permute-done | bytes 332832
  592.5 1.9 collective-permute-start.6
  595.2 11.5 %collective-permute-done.2 = bf16[64,3200]{1,0:T(8,128)(2,1)S(1)} collective-permute-done((bf16[64,3200]{1,0:T(8,128)(2,1)S(1)}, bf16[64,3200]{1,0:T(8,128)(2,1)S(1)}, u32[]{:S(2)}, u32[]{:S(2)}) %collective-permute-start.2) | collective-permute-done | bytes 409632
  608.5 39.1 %collective-permute-done.6 = bf16[64,3200]{1,0:T(8,128)(2,1)} collective-permute-done((bf16[64,3200]{1,0:T(8,128)(2,1)S(1)}, bf16[64,3200]{1,0:T(8,128)(2,1)}, u32[]{:S(2)}, u32[]{:S(2)}) %collective-permute-start.6) | collective-permute-done | bytes 409632
  647.6 21.1 %concatenate = bf16[436,3200]{1,0:T(8,128)(2,1)S(1)} concatenate(bf16[52,3200]{1,0:T(8,128)(2,1)} %copy-done.5, bf16[64,3200]{1,0:T(8,128)(2,1)} %collective-permute-done.6, bf16[64,3200]{1,0:T(8,128)(2,1)} %copy-done.4, bf16[64,3200]{1,0:T(8,128)(2,1)} %copy-done.3, bf16[64,3200]{1,0:T(8,128)(2,1)} %copy-done.2, bf16[64,3200]{1,0:T(8,128)(2,1)} %copy-done.1, ...), dimensions={0} | concatenate | bytes 5580800
  (183 shorter events, 60.5 us)
Async XLA Ops:
  7.2 165.5 %all-gather.6.cloned.1.call-start = ((), (), s32[]{:S(2)}) async-start(), calls=%async_computation | async-start | bytes 21964800 | tf_op jit(solution)/shard_map/all_gather | solution.py:70
  188.0 8.5 %copy-start = (f32[1,1664]{1,0:T(1,128)S(1)}, f32[1,1664]{1,0:T(1,128)}, u32[]{:S(2)}) copy-start(f32[1,1664]{1,0:T(1,128)} %param.20) | copy-start | bytes 19972
  201.2 11.8 %collective-permute-start = (bf16[32,3200]{1,0:T(8,128)(2,1)S(1)}, bf16[32,3200]{1,0:T(8,128)(2,1)S(1)}, u32[]{:S(2)}, u32[]{:S(2)}) collective-permute-start(bf16[32,3200]{1,0:T(8,128)(2,1)S(1)} %get-tuple-element.384), channel_id=1, source_target_pairs={{64,0},{128,64},{192,128},{65,1},{129,65},{193,129},{66,2},{130,66... | collective-permute-start | bytes 614408 | tf_op jit(solution)/shard_map/while/body/eval_jaxpr/ppermute | solution.py:22
  205.1 7.8 %collective-permute-start.1 = (bf16[32,1664]{1,0:T(8,128)(2,1)S(1)}, bf16[32,1664]{1,0:T(8,128)(2,1)S(1)}, u32[]{:S(2)}, u32[]{:S(2)}) collective-permute-start(bf16[32,1664]{1,0:T(8,128)(2,1)S(1)} %get-tuple-element.385), channel_id=1, source_target_pairs={{64,0},{128,64},{192,128},{65,1},{129,65},{193,129},{66,2},{130,66... | collective-permute-start | bytes 319496 | tf_op jit(solution)/shard_map/while/body/eval_jaxpr/ppermute | solution.py:22
  217.6 11.8 %collective-permute-start = (bf16[32,3200]{1,0:T(8,128)(2,1)S(1)}, bf16[32,3200]{1,0:T(8,128)(2,1)S(1)}, u32[]{:S(2)}, u32[]{:S(2)}) collective-permute-start(bf16[32,3200]{1,0:T(8,128)(2,1)S(1)} %get-tuple-element.384), channel_id=1, source_target_pairs={{64,0},{128,64},{192,128},{65,1},{129,65},{193,129},{66,2},{130,66... | collective-permute-start | bytes 614408 | tf_op jit(solution)/shard_map/while/body/eval_jaxpr/ppermute | solution.py:22
  221.6 7.8 %collective-permute-start.1 = (bf16[32,1664]{1,0:T(8,128)(2,1)S(1)}, bf16[32,1664]{1,0:T(8,128)(2,1)S(1)}, u32[]{:S(2)}, u32[]{:S(2)}) collective-permute-start(bf16[32,1664]{1,0:T(8,128)(2,1)S(1)} %get-tuple-element.385), channel_id=1, source_target_pairs={{64,0},{128,64},{192,128},{65,1},{129,65},{193,129},{66,2},{130,66... | collective-permute-start | bytes 319496 | tf_op jit(solution)/shard_map/while/body/eval_jaxpr/ppermute | solution.py:22
  234.1 28.9 %collective-permute-start = (bf16[32,3200]{1,0:T(8,128)(2,1)S(1)}, bf16[32,3200]{1,0:T(8,128)(2,1)S(1)}, u32[]{:S(2)}, u32[]{:S(2)}) collective-permute-start(bf16[32,3200]{1,0:T(8,128)(2,1)S(1)} %get-tuple-element.384), channel_id=1, source_target_pairs={{64,0},{128,64},{192,128},{65,1},{129,65},{193,129},{66,2},{130,66... | collective-permute-start | bytes 614408 | tf_op jit(solution)/shard_map/while/body/eval_jaxpr/ppermute | solution.py:22
  238.0 24.9 %collective-permute-start.1 = (bf16[32,1664]{1,0:T(8,128)(2,1)S(1)}, bf16[32,1664]{1,0:T(8,128)(2,1)S(1)}, u32[]{:S(2)}, u32[]{:S(2)}) collective-permute-start(bf16[32,1664]{1,0:T(8,128)(2,1)S(1)} %get-tuple-element.385), channel_id=1, source_target_pairs={{64,0},{128,64},{192,128},{65,1},{129,65},{193,129},{66,2},{130,66... | collective-permute-start | bytes 319496 | tf_op jit(solution)/shard_map/while/body/eval_jaxpr/ppermute | solution.py:22
  275.5 23.8 %collective-permute-start = (bf16[32,3200]{1,0:T(8,128)(2,1)S(1)}, bf16[32,3200]{1,0:T(8,128)(2,1)S(1)}, u32[]{:S(2)}, u32[]{:S(2)}) collective-permute-start(bf16[32,3200]{1,0:T(8,128)(2,1)S(1)} %get-tuple-element.384), channel_id=1, source_target_pairs={{64,0},{128,64},{192,128},{65,1},{129,65},{193,129},{66,2},{130,66... | collective-permute-start | bytes 614408 | tf_op jit(solution)/shard_map/while/body/eval_jaxpr/ppermute | solution.py:22
  279.5 19.9 %collective-permute-start.1 = (bf16[32,1664]{1,0:T(8,128)(2,1)S(1)}, bf16[32,1664]{1,0:T(8,128)(2,1)S(1)}, u32[]{:S(2)}, u32[]{:S(2)}) collective-permute-start(bf16[32,1664]{1,0:T(8,128)(2,1)S(1)} %get-tuple-element.385), channel_id=1, source_target_pairs={{64,0},{128,64},{192,128},{65,1},{129,65},{193,129},{66,2},{130,66... | collective-permute-start | bytes 319496 | tf_op jit(solution)/shard_map/while/body/eval_jaxpr/ppermute | solution.py:22
  312.0 23.8 %collective-permute-start = (bf16[32,3200]{1,0:T(8,128)(2,1)S(1)}, bf16[32,3200]{1,0:T(8,128)(2,1)S(1)}, u32[]{:S(2)}, u32[]{:S(2)}) collective-permute-start(bf16[32,3200]{1,0:T(8,128)(2,1)S(1)} %get-tuple-element.384), channel_id=1, source_target_pairs={{64,0},{128,64},{192,128},{65,1},{129,65},{193,129},{66,2},{130,66... | collective-permute-start | bytes 614408 | tf_op jit(solution)/shard_map/while/body/eval_jaxpr/ppermute | solution.py:22
  315.9 19.9 %collective-permute-start.1 = (bf16[32,1664]{1,0:T(8,128)(2,1)S(1)}, bf16[32,1664]{1,0:T(8,128)(2,1)S(1)}, u32[]{:S(2)}, u32[]{:S(2)}) collective-permute-start(bf16[32,1664]{1,0:T(8,128)(2,1)S(1)} %get-tuple-element.385), channel_id=1, source_target_pairs={{64,0},{128,64},{192,128},{65,1},{129,65},{193,129},{66,2},{130,66... | collective-permute-start | bytes 319496 | tf_op jit(solution)/shard_map/while/body/eval_jaxpr/ppermute | solution.py:22
  348.4 23.8 %collective-permute-start = (bf16[32,3200]{1,0:T(8,128)(2,1)S(1)}, bf16[32,3200]{1,0:T(8,128)(2,1)S(1)}, u32[]{:S(2)}, u32[]{:S(2)}) collective-permute-start(bf16[32,3200]{1,0:T(8,128)(2,1)S(1)} %get-tuple-element.384), channel_id=1, source_target_pairs={{64,0},{128,64},{192,128},{65,1},{129,65},{193,129},{66,2},{130,66... | collective-permute-start | bytes 614408 | tf_op jit(solution)/shard_map/while/body/eval_jaxpr/ppermute | solution.py:22
  352.3 19.9 %collective-permute-start.1 = (bf16[32,1664]{1,0:T(8,128)(2,1)S(1)}, bf16[32,1664]{1,0:T(8,128)(2,1)S(1)}, u32[]{:S(2)}, u32[]{:S(2)}) collective-permute-start(bf16[32,1664]{1,0:T(8,128)(2,1)S(1)} %get-tuple-element.385), channel_id=1, source_target_pairs={{64,0},{128,64},{192,128},{65,1},{129,65},{193,129},{66,2},{130,66... | collective-permute-start | bytes 319496 | tf_op jit(solution)/shard_map/while/body/eval_jaxpr/ppermute | solution.py:22
  384.8 22.6 %collective-permute-start = (bf16[32,3200]{1,0:T(8,128)(2,1)S(1)}, bf16[32,3200]{1,0:T(8,128)(2,1)S(1)}, u32[]{:S(2)}, u32[]{:S(2)}) collective-permute-start(bf16[32,3200]{1,0:T(8,128)(2,1)S(1)} %get-tuple-element.384), channel_id=1, source_target_pairs={{64,0},{128,64},{192,128},{65,1},{129,65},{193,129},{66,2},{130,66... | collective-permute-start | bytes 614408 | tf_op jit(solution)/shard_map/while/body/eval_jaxpr/ppermute | solution.py:22
  388.7 18.6 %collective-permute-start.1 = (bf16[32,1664]{1,0:T(8,128)(2,1)S(1)}, bf16[32,1664]{1,0:T(8,128)(2,1)S(1)}, u32[]{:S(2)}, u32[]{:S(2)}) collective-permute-start(bf16[32,1664]{1,0:T(8,128)(2,1)S(1)} %get-tuple-element.385), channel_id=1, source_target_pairs={{64,0},{128,64},{192,128},{65,1},{129,65},{193,129},{66,2},{130,66... | collective-permute-start | bytes 319496 | tf_op jit(solution)/shard_map/while/body/eval_jaxpr/ppermute | solution.py:22
  407.3 163.6 %copy-start.6 = (u32[256]{0:T(256)S(1)}, u32[256]{0:T(256)}, u32[]{:S(2)}) copy-start(u32[256]{0:T(256)} %constant.134) | copy-start | bytes 3076
  568.2 24.3 %collective-permute-start.7 = (bf16[52,3200]{1,0:T(8,128)(2,1)S(1)}, bf16[52,3200]{1,0:T(8,128)(2,1)S(1)}, u32[]{:S(2)}, u32[]{:S(2)}) collective-permute-start(bf16[52,3200]{1,0:T(8,128)(2,1)S(1)} %slice.4), channel_id=1, source_target_pairs={{0,12},{2,14},{4,16},{6,18},{8,20},{10,22},{12,24},{14,26},{16,28}... | collective-permute-start | bytes 998408
  572.1 34.5 %collective-permute-start.2 = (bf16[64,3200]{1,0:T(8,128)(2,1)S(1)}, bf16[64,3200]{1,0:T(8,128)(2,1)S(1)}, u32[]{:S(2)}, u32[]{:S(2)}) collective-permute-start(bf16[64,3200]{1,0:T(8,128)(2,1)S(1)} %fusion), channel_id=1, source_target_pairs={{0,2},{2,4},{4,6},{6,8},{8,10},{10,12},{12,14},{14,16},{16,18},{18... | collective-permute-start | bytes 1228808
  574.1 32.6 %collective-permute-start.3 = (bf16[64,3200]{1,0:T(8,128)(2,1)S(1)}, bf16[64,3200]{1,0:T(8,128)(2,1)S(1)}, u32[]{:S(2)}, u32[]{:S(2)}) collective-permute-start(bf16[64,3200]{1,0:T(8,128)(2,1)S(1)} %fusion), channel_id=1, source_target_pairs={{0,4},{2,6},{4,8},{6,10},{8,12},{10,14},{12,16},{14,18},{16,20},{1... | collective-permute-start | bytes 1228808
  579.9 26.8 %collective-permute-start.4 = (bf16[64,3200]{1,0:T(8,128)(2,1)S(1)}, bf16[64,3200]{1,0:T(8,128)(2,1)S(1)}, u32[]{:S(2)}, u32[]{:S(2)}) collective-permute-start(bf16[64,3200]{1,0:T(8,128)(2,1)S(1)} %fusion), channel_id=1, source_target_pairs={{0,6},{2,8},{4,10},{6,12},{8,14},{10,16},{12,18},{14,20},{16,22},{... | collective-permute-start | bytes 1228808
  581.8 24.9 %collective-permute-start.5 = (bf16[64,3200]{1,0:T(8,128)(2,1)S(1)}, bf16[64,3200]{1,0:T(8,128)(2,1)S(1)}, u32[]{:S(2)}, u32[]{:S(2)}) collective-permute-start(bf16[64,3200]{1,0:T(8,128)(2,1)S(1)} %fusion), channel_id=1, source_target_pairs={{0,8},{2,10},{4,12},{6,14},{8,16},{10,18},{12,20},{14,22},{16,24},... | collective-permute-start | bytes 1228808
  592.5 14.2 %copy-start.5 = (bf16[52,3200]{1,0:T(8,128)(2,1)}, bf16[52,3200]{1,0:T(8,128)(2,1)S(1)}, u32[]{:S(2)}) copy-start(bf16[52,3200]{1,0:T(8,128)(2,1)S(1)} %collective-permute-done.7) | copy-start | bytes 998404
  592.5 55.1 %collective-permute-start.6 = (bf16[64,3200]{1,0:T(8,128)(2,1)S(1)}, bf16[64,3200]{1,0:T(8,128)(2,1)}, u32[]{:S(2)}, u32[]{:S(2)}) collective-permute-start(bf16[64,3200]{1,0:T(8,128)(2,1)S(1)} %fusion), channel_id=1, source_target_pairs={{0,10},{2,12},{4,14},{6,16},{8,18},{10,20},{12,22},{14,24},{16,26}... | collective-permute-start | bytes 1228808
  606.6 0.8 copy-start.1
  606.7 0.9 copy-start.2
  606.7 1.0 copy-start.3
  607.7 0.7 copy-start.4
Sparse Core Ops, SparseCore 0:
  10.6 161.9 all-gather.5
